TPU v7x, 512 devices: a whole 4x4x16 slice. The times are simulated.
512 devices in a mesh: ctx: 32 (over z, core), exp: 16 (over y, x).
Axes of the slice: x: 4, y: 4, z: 16, core: 2. Of those that a mesh axis runs over, the one named last changes fastest.
Arguments:
- x_in: bfloat16 [4096, 4096], P('ctx', 'exp'), may hold values from -6 to 6
- z_gate: bfloat16 [4096, 4096], P('ctx', 'exp'), may hold values from -6 to 6
- b_proj: bfloat16 [4096, 128], P('ctx'), may hold values from -0.5 to 0.5
- c_proj: bfloat16 [4096, 128], P('ctx'), may hold values from -0.5 to 0.5
- dt_raw: float32 [64, 4096], P('exp', 'ctx'), may hold values from -4 to 4
- a_log: float32 [64], P('exp'), may hold values from -13 to -2.9
- d_skip: float32 [64], P('exp'), may hold values from 0.5 to 1.5
- out_proj: bfloat16 [4096, 2048], P('exp'), may hold values from -0.09375 to 0.09375
- residual: bfloat16 [4096, 2048], P('ctx'), may hold values from -80 to 80
- norm_gain: float32 [2048], replicated, may hold values from 0.5 to 1.5
- router: bfloat16 [2048, 16], replicated, may hold values from -0.125 to 0.125
- w_gate: bfloat16 [16, 2048, 7168], P(None, 'ctx', 'exp'), may hold values from -0.125 to 0.125
- w_up: bfloat16 [16, 2048, 7168], P(None, 'ctx', 'exp'), may hold values from -0.125 to 0.125
- w_down: bfloat16 [16, 2048, 7168], P(None, 'ctx', 'exp'), may hold values from -0.0625 to 0.0625
- block_experts: int32 [32, 2], replicated, may hold values from 0 to 15, all different within a row
Outputs:
- stream_out: bfloat16 [4096, 2048], P('ctx', 'exp')
- expert_out: bfloat16 [4096, 2048], P('ctx', 'exp')
All inputs are finite; a program needn't handle non-finite values.
Results may differ from a plain program's by a relative error of at most 0.03.
Values may be sent and summed in bfloat16 or wider, within the bound.
A program may use at most 64 MiB of HBM per device.

v0:
```python
import jax
import jax.numpy as jnp
from jax import lax
from jax.sharding import PartitionSpec as P

BLOCK = 128
highest = lax.Precision.HIGHEST
epsilon = 1e-05


def shifted(shard, axis, by):
    size = lax.axis_size(axis)
    pairs = [(i, i + by) for i in range(size) if 0 <= i + by < size]
    return lax.ppermute(shard, axis, pairs)


def block_terms(inputs_f, steps_f, keys_f, queries_f, head_rates):
    length = inputs_f.shape[0]
    log_decay = -head_rates[:, None] * steps_f
    running = jnp.cumsum(log_decay, axis=1)
    spread = running[:, :, None] - running[:, None, :]
    lower_part = jnp.arange(length)[:, None] >= jnp.arange(length)[None, :]
    weights = jnp.where(lower_part[None], jnp.exp(jnp.minimum(spread, 0.0)), 0.0)
    scores = jnp.dot(queries_f, keys_f.T, precision=highest)
    mixing = scores[None] * weights * steps_f[:, None, :]
    inside = jnp.einsum("hls,shp->lhp", mixing, inputs_f, precision=highest)
    carry_weight = jnp.exp(running[:, -1:] - running) * steps_f
    own_state = jnp.einsum("hs,shp,sn->hpn", carry_weight, inputs_f, keys_f, precision=highest)
    return (inside, own_state, jnp.exp(running), jnp.exp(running[:, -1]))


def per_device(
    x_in,
    z_gate,
    b_proj,
    c_proj,
    dt_raw,
    a_log,
    d_skip,
    out_proj,
    residual,
    norm_gain,
    router,
    w_gate,
    w_up,
    w_down,
    block_experts,
):
    slab_rows = x_in.shape[0]
    head_count = dt_raw.shape[0]
    head_size = x_in.shape[1] // head_count
    blocks_here = slab_rows // BLOCK
    head_rates = jnp.exp(a_log)
    steps_f = jax.nn.softplus(dt_raw).reshape(head_count, blocks_here, BLOCK).transpose(1, 0, 2)
    inputs_f = x_in.astype(jnp.float32).reshape(blocks_here, BLOCK, head_count, head_size)
    keys_f = b_proj.astype(jnp.float32).reshape(blocks_here, BLOCK, -1)
    queries_f = c_proj.astype(jnp.float32).reshape(blocks_here, BLOCK, -1)
    inside, own_state, entry_scale, block_decay = jax.vmap(block_terms, in_axes=(0, 0, 0, 0, None))(
        inputs_f, steps_f, keys_f, queries_f, head_rates
    )
    partial_states = []
    slab_keep = jnp.ones((head_count,), jnp.float32)
    slab_state = jnp.zeros(own_state.shape[1:], jnp.float32)
    kept_decay = slab_keep
    partial_states.append(slab_state)
    slab_state = block_decay[0][:, None, None] * slab_state + own_state[0]
    slab_keep = slab_keep * block_decay[0]

    def relay(turn, arriving):
        return shifted(
            (slab_keep[:, None, None] * arriving + slab_state).astype(jnp.bfloat16), "ctx", 1
        ).astype(jnp.float32)

    incoming = lax.fori_loop(0, lax.axis_size("ctx") - 1, relay, jnp.zeros_like(slab_state))
    entering = jnp.stack([kept_decay[:, None, None] * incoming])
    from_before = entry_scale.transpose(0, 2, 1)[..., None] * jnp.einsum(
        "bln,bhpn->blhp", queries_f, entering, precision=highest
    )
    outputs = inside + from_before + d_skip[None, None, :, None] * inputs_f
    gated_rows = (outputs.reshape(slab_rows, -1) * jax.nn.silu(z_gate.astype(jnp.float32))).astype(
        jnp.bfloat16
    )
    group_term = jnp.dot(gated_rows, out_proj, preferred_element_type=jnp.float32).astype(
        jnp.bfloat16
    )
    model_width = residual.shape[1]
    share_cols = model_width // lax.axis_size("exp")
    first_col = lax.axis_index("exp") * share_cols
    mixed_sum = lax.psum(group_term, "exp").astype(jnp.float32)
    stream_full = mixed_sum + residual.astype(jnp.float32)
    mean_square = jnp.mean(stream_full * stream_full, axis=1, keepdims=True)
    normed = (stream_full * lax.rsqrt(mean_square + epsilon) * norm_gain).astype(jnp.bfloat16)
    stream_share = lax.dynamic_slice_in_dim(stream_full, first_col, share_cols, 1)
    expert_count = router.shape[1]
    logits = jnp.dot(normed, router, preferred_element_type=jnp.float32).reshape(
        blocks_here, BLOCK, expert_count
    )
    named_here = lax.dynamic_slice_in_dim(
        block_experts, lax.axis_index("ctx") * blocks_here, blocks_here, 0
    )
    one_hot = (
        named_here[:, :, None] == jnp.arange(expert_count, dtype=jnp.int32)[None, None, :]
    ).astype(jnp.float32)
    chosen = jnp.einsum("bte,bse->bts", logits, one_hot, precision=highest)
    mixing_gates = jax.nn.sigmoid(chosen - chosen[:, :, ::-1])
    flat_named = block_experts.reshape(-1)
    sent_gate = jnp.take(w_gate, flat_named, axis=0)
    sent_up = jnp.take(w_up, flat_named, axis=0)
    sent_down = jnp.take(w_down, flat_named, axis=0)
    got_gate, got_up, got_down = (
        lax.all_to_all(sent_gate, "ctx", split_axis=0, concat_axis=1, tiled=True),
        lax.all_to_all(sent_up, "ctx", split_axis=0, concat_axis=1, tiled=True),
        lax.all_to_all(sent_down, "ctx", split_axis=0, concat_axis=1, tiled=True),
    )
    full_gate = got_gate.reshape(blocks_here, 2, model_width, -1)
    full_up = got_up.reshape(blocks_here, 2, model_width, -1)
    full_down = got_down.reshape(blocks_here, 2, model_width, -1)
    rows_in = normed.reshape(blocks_here, BLOCK, model_width)
    gate_part = jnp.einsum("btd,bkdf->bktf", rows_in, full_gate, preferred_element_type=jnp.float32)
    up_part = jnp.einsum("btd,bkdf->bktf", rows_in, full_up, preferred_element_type=jnp.float32)
    hidden = (jax.nn.silu(gate_part) * up_part).astype(jnp.bfloat16)
    down_part = jnp.einsum("bktf,bkdf->bktd", hidden, full_down, preferred_element_type=jnp.float32)
    weighted = jnp.sum(mixing_gates.transpose(0, 2, 1)[..., None] * down_part, axis=1).reshape(
        slab_rows, model_width
    )
    expert_share = lax.psum_scatter(
        weighted.astype(jnp.bfloat16), "exp", scatter_dimension=1, tiled=True
    )
    return (stream_share.astype(jnp.bfloat16), expert_share)


def solution(mesh):
    placed = (
        P("ctx", "exp"),
        P("ctx", "exp"),
        P("ctx", None),
        P("ctx", None),
        P("exp", "ctx"),
        P("exp"),
        P("exp"),
        P("exp", None),
        P("ctx", None),
        P(),
        P(),
        P(None, "ctx", "exp"),
        P(None, "ctx", "exp"),
        P(None, "ctx", "exp"),
        P(),
    )
    return jax.shard_map(
        per_device,
        mesh=mesh,
        in_specs=placed,
        out_specs=(P("ctx", "exp"), P("ctx", "exp")),
        check_vma=False,
    )
```

profile of v0, /device:TPU:2, one launch (start us, length us, event | category | flops | bytes accessed | tf_op | source)
XLA Modules:
  0.0 1058.6 jit_solution(5072608627155439137)
XLA Ops:
  8.4 2.8 gather_fusion.2
  11.2 2.8 gather_fusion.1
  14.0 2.8 gather_fusion
  16.7 7.0 broadcast_select_fusion.2
  23.7 206.2 %all_to_all.45 = bf16[64,64,448]{2,1,0:T(8,128)(2,1)} all-to-all(bf16[64,64,448]{2,1,0:T(8,128)(2,1)S(1)} %get-tuple-element.53), channel_id=1, replica_groups=mesh['ctx'=32,'exp'=16] {'ctx'}, dimensions={0} | all-to-all | bytes 7340032 | tf_op jit(solution)/shard_map/all_to_all | solution.py:111
  229.9 195.0 %all_to_all.46 = bf16[64,64,448]{2,1,0:T(8,128)(2,1)} all-to-all(bf16[64,64,448]{2,1,0:T(8,128)(2,1)S(1)} %get-tuple-element.54), channel_id=1, replica_groups=mesh['ctx'=32,'exp'=16] {'ctx'}, dimensions={0} | all-to-all | bytes 7340032 | tf_op jit(solution)/shard_map/all_to_all | solution.py:112
  425.0 5.0 all-to-all-start.2
  431.3 364.5 %while.11 = (s32[]{:T(128)}, f32[4,64,128]{2,1,0:T(8,128)S(1)}, f32[1,4]{1,0:T(1,128)S(1)}, f32[4,64,128]{2,1,0:T(8,128)S(1)}, s32[]{:T(128)}, /*index=5*/s32[]{:T(128)}) while((s32[]{:T(128)}, f32[4,64,128]{2,1,0:T(8,128)S(1)}, f32[1,4]{1,0:T(1,128)S(1)}, f32[4,64,128]{2,1,0:T(8,128)S(1)}, s32[]{:T(128)}, ...), condition=%wide.region_2.3_spmd.clone, body=%wide.region_1.2_spmd.clone.sunk | while | flops 163843 | bytes 786567 | solution.py:74
  431.4 2.0 collective-permute-start
  433.4 0.9 collective-permute-done
  434.4 171.0 %collective-permute-start = (bf16[4,64,128]{2,1,0:T(8,128)(2,1)S(1)}, bf16[4,64,128]{2,1,0:T(8,128)(2,1)S(1)}, u32[]{:S(2)}, u32[]{:S(2)}) collective-permute-start(bf16[4,64,128]{2,1,0:T(8,128)(2,1)S(1)} %fusion.64), channel_id=1, source_target_pairs={{0,16},{16,32},{32,48},{48,64},{64,80},{80,96},{96,112},{112,128},... | collective-permute-start | bytes 196616 | tf_op jit(solution)/shard_map/while/body/eval_jaxpr/ppermute | solution.py:14
  605.4 0.9 collective-permute-done
  606.4 10.2 collective-permute-start
  616.7 0.9 collective-permute-done
  617.7 4.8 collective-permute-start
  622.5 0.9 collective-permute-done
  623.5 4.7 collective-permute-start
  628.2 0.9 collective-permute-done
  629.2 4.7 collective-permute-start
  633.9 0.9 collective-permute-done
  634.9 4.7 collective-permute-start
  640.6 4.7 collective-permute-start
  646.3 4.7 collective-permute-start
  652.1 4.7 collective-permute-start
  656.8 0.9 collective-permute-done
  657.8 4.7 collective-permute-start
  662.5 0.9 collective-permute-done
  663.5 4.7 collective-permute-start
  668.2 0.9 collective-permute-done
  669.2 4.7 collective-permute-start
  673.9 0.9 collective-permute-done
  674.9 4.7 collective-permute-start
  679.6 0.9 collective-permute-done
  680.6 4.7 collective-permute-start
  685.3 0.9 collective-permute-done
  686.3 4.9 collective-permute-start
  691.2 0.9 collective-permute-done
  692.2 5.9 collective-permute-start
  699.1 5.9 collective-permute-start
  706.0 5.9 collective-permute-start
  712.9 5.9 collective-permute-start
  719.8 5.9 collective-permute-start
  726.7 5.9 collective-permute-start
  733.7 5.9 collective-permute-start
  740.6 5.9 collective-permute-start
  747.5 5.9 collective-permute-start
  754.4 5.9 collective-permute-start
  761.3 5.9 collective-permute-start
  768.2 5.9 collective-permute-start
  775.2 5.9 collective-permute-start
  782.1 5.9 collective-permute-start
  789.0 5.9 collective-permute-start
  796.8 1.1 convolution_convert_fusion
  798.2 140.2 %all-reduce.2.cloned.1.call-done = bf16[128,2048]{1,0:T(8,128)(2,1)} async-done(((bf16[128,2048]{1,0:T(8,128)(2,1)}), bf16[128,2048]{1,0:T(8,128)(2,1)}) %all-reduce.2.cloned.1.call-update) | async-done | bytes 524304 | tf_op jit(solution)/shard_map/psum | solution.py:89
  938.4 1.3 multiply_reduce_fusion
  939.8 1.3 multiply_convert_fusion
  941.5 2.8 copy.39
  945.0 2.5 copy.41
  947.5 2.1 convolution_bitcast_fusion.1
  949.5 4.7 copy.43
  954.2 7.9 fusion.2
  962.0 1.0 copy.48
  963.9 86.5 %reduce-scatter.4.cloned.1.call-done = bf16[128,128]{1,0:T(8,128)(2,1)} async-done(((bf16[2048,128]{1,0:T(8,128)(2,1)}), bf16[128,128]{1,0:T(8,128)(2,1)}) %reduce-scatter.4.cloned.1.call-update) | async-done | bytes 32784
  1050.3 1.5 copy.49
  (148 shorter events, 24.4 us)
Async XLA Ops:
  7.2 1.2 copy-start
  8.4 2.8 copy-start.2
  11.2 2.8 copy-start.3
  424.9 5.2 copy-start.7
  424.9 5.4 copy-start.15
  424.9 5.4 copy-start.13
  424.9 6.1 copy-start.8
  424.9 370.9 %copy-start.9 = (bf16[128,128]{1,0:T(8,128)(2,1)S(1)}, bf16[128,128]{1,0:T(8,128)(2,1)}, u32[]{:S(2)}) copy-start(bf16[128,128]{1,0:T(8,128)(2,1)} %param.22) | copy-start | bytes 98308
  424.9 371.3 %copy-start.16 = (f32[4]{0:T(128)S(1)}, f32[4]{0:T(128)}, u32[]{:S(2)}) copy-start(f32[4]{0:T(128)} %param.25) | copy-start | bytes 52
  425.0 524.6 %all-to-all-start.2 = ((bf16[64,64,448]{2,1,0:T(8,128)(2,1)}), bf16[64,64,448]{2,1,0:T(8,128)(2,1)}, u32[]{:S(2)}, u32[]{:S(2)}) async-start(bf16[64,64,448]{2,1,0:T(8,128)(2,1)} %get-tuple-element.55), calls=%async_computation.2 | async-start | bytes 8388608 | tf_op jit(solution)/shard_map/all_to_all | solution.py:113
  430.0 366.9 %copy-start.6 = (bf16[256,2048]{1,0:T(8,128)(2,1)S(1)}, bf16[256,2048]{1,0:T(8,128)(2,1)}, u32[]{:S(2)}) copy-start(bf16[256,2048]{1,0:T(8,128)(2,1)} %param.26) | copy-start | bytes 3145732
  430.0 366.9 %copy-start.10 = (bf16[128,256]{1,0:T(8,128)(2,1)S(1)}, bf16[128,256]{1,0:T(8,128)(2,1)}, u32[]{:S(2)}) copy-start(bf16[128,256]{1,0:T(8,128)(2,1)} %param.20) | copy-start | bytes 196612
  430.0 368.1 %copy-start.14 = (s32[32,2]{0,1:T(2,128)S(1)}, s32[32,2]{0,1:T(2,128)}, u32[]{:S(2)}) copy-start(s32[32,2]{0,1:T(2,128)} %param.33) | copy-start | bytes 772
  430.0 508.4 %copy-start.4 = (bf16[128,2048]{1,0:T(8,128)(2,1)S(1)}, bf16[128,2048]{1,0:T(8,128)(2,1)}, u32[]{:S(2)}) copy-start(bf16[128,2048]{1,0:T(8,128)(2,1)} %param.27) | copy-start | bytes 1572868
  430.0 509.7 %copy-start.12 = (f32[2048]{0:T(1024)S(1)}, f32[2048]{0:T(1024)}, u32[]{:S(2)}) copy-start(f32[2048]{0:T(1024)} %param.28) | copy-start | bytes 24580
  430.0 508.4 %all-reduce.2.cloned.1.call-start = ((), (), s32[]{:S(2)}) async-start(), calls=%async_computation.4 | async-start | bytes 1048576 | tf_op jit(solution)/shard_map/psum | solution.py:89
  431.3 509.7 %copy-start.11 = (bf16[2048,16]{0,1:T(8,128)(2,1)S(1)}, bf16[2048,16]{0,1:T(8,128)(2,1)}, u32[]{:S(2)}) copy-start(bf16[2048,16]{0,1:T(8,128)(2,1)} %param.29) | copy-start | bytes 196612
  431.4 2.9 collective-permute-start
  434.4 171.9 %collective-permute-start = (bf16[4,64,128]{2,1,0:T(8,128)(2,1)S(1)}, bf16[4,64,128]{2,1,0:T(8,128)(2,1)S(1)}, u32[]{:S(2)}, u32[]{:S(2)}) collective-permute-start(bf16[4,64,128]{2,1,0:T(8,128)(2,1)S(1)} %fusion.64), channel_id=1, source_target_pairs={{0,16},{16,32},{32,48},{48,64},{64,80},{80,96},{96,112},{112,128},... | collective-permute-start | bytes 196616 | tf_op jit(solution)/shard_map/while/body/eval_jaxpr/ppermute | solution.py:14
  606.4 11.1 %collective-permute-start = (bf16[4,64,128]{2,1,0:T(8,128)(2,1)S(1)}, bf16[4,64,128]{2,1,0:T(8,128)(2,1)S(1)}, u32[]{:S(2)}, u32[]{:S(2)}) collective-permute-start(bf16[4,64,128]{2,1,0:T(8,128)(2,1)S(1)} %fusion.64), channel_id=1, source_target_pairs={{0,16},{16,32},{32,48},{48,64},{64,80},{80,96},{96,112},{112,128},... | collective-permute-start | bytes 196616 | tf_op jit(solution)/shard_map/while/body/eval_jaxpr/ppermute | solution.py:14
  617.7 5.7 collective-permute-start
  623.5 5.6 collective-permute-start
  629.2 5.6 collective-permute-start
  634.9 5.6 collective-permute-start
  640.6 5.6 collective-permute-start
  646.3 5.6 collective-permute-start
  652.1 5.6 collective-permute-start
  657.8 5.6 collective-permute-start
  663.5 5.6 collective-permute-start
  669.2 5.6 collective-permute-start
  674.9 5.6 collective-permute-start
  680.6 5.6 collective-permute-start
  686.3 5.7 collective-permute-start
  692.2 6.8 collective-permute-start
  699.1 6.8 collective-permute-start
  706.0 6.8 collective-permute-start
  712.9 6.8 collective-permute-start
  719.8 6.8 collective-permute-start
  726.7 6.8 collective-permute-start
  733.7 6.8 collective-permute-start
  740.6 6.8 collective-permute-start
  747.5 6.8 collective-permute-start
  754.4 6.8 collective-permute-start
  761.3 6.8 collective-permute-start
  768.2 6.8 collective-permute-start
  775.2 6.8 collective-permute-start
  782.1 6.8 collective-permute-start
  789.0 6.8 collective-permute-start
  798.0 252.3 %reduce-scatter.4.cloned.1.call-start = ((), (), s32[]{:S(2)}) async-start(), calls=%async_computation.5 | async-start | bytes 557056
  941.5 3.5 copy-start.1
  954.2 8.9 copy-start.5
Sparse Core Ops, SparseCore 0:
  798.1 140.2 all-reduce.1
  963.2 87.0 reduce-scatter.3
where the time goes:
time: 1060 us
  blocking collectives  401 us (38%)
  starting transfers between devices  338 us (32%)
  waiting for transfers between devices  254 us (24%)
  local copies, waits for them, and re-layouts  24 us (2%)
  between operations  14.4 us (1%)
  other arithmetic  13.2 us (1%)
  matrix products  12.6 us (1%)
    ppermute x31, starting transfers between devices, shifted(): return lax.ppermute(shard, axis, pairs)  333 us
    all_to_all x1, blocking collectives, per_device(): lax.all_to_all(sent_gate, 'ctx', split_axis=0, concat_axis=1, tiled=True)  206 us
    all_to_all x1, blocking collectives, per_device(): lax.all_to_all(sent_up, 'ctx', split_axis=0, concat_axis=1, tiled=True)  195 us
    psum x1, waiting for transfers between devices, per_device(): mixed_sum = lax.psum(group_term, 'exp').astype(jnp.float32)  140 us
    unnamed x3, waiting for transfers between devices  86.5 us
    ppermute x31, waiting for transfers between devices, shifted(): return lax.ppermute(shard, axis, pairs)  27.3 us
  transfers between devices with their start and end apart: 34, of which 33 were waited for; matrix products, arithmetic and copies ran while one was open for 2% of the time, Pallas kernels for 0%

commit v1 on v0

--- a/solution.py
+++ b/solution.py
@@ -2,6 +2,7 @@
 import jax.numpy as jnp
 from jax import lax
 from jax.sharding import PartitionSpec as P
+from jax.lax import all_gather
 
 BLOCK = 128
 highest = lax.Precision.HIGHEST
@@ -86,7 +87,11 @@
     model_width = residual.shape[1]
     share_cols = model_width // lax.axis_size("exp")
     first_col = lax.axis_index("exp") * share_cols
-    mixed_sum = lax.psum(group_term, "exp").astype(jnp.float32)
+
+    def layers_all_change(here_x):
+        return all_gather(here_x, axis_name="exp").sum(axis=0)
+
+    mixed_sum = layers_all_change(group_term).astype(jnp.float32)
     stream_full = mixed_sum + residual.astype(jnp.float32)
     mean_square = jnp.mean(stream_full * stream_full, axis=1, keepdims=True)
     normed = (stream_full * lax.rsqrt(mean_square + epsilon) * norm_gain).astype(jnp.bfloat16)

time: 1060 us -> 943 us (0.89)
  blocking collectives: 401 us -> 206 us
  starting transfers between devices: 338 us -> 374 us
  waiting for transfers between devices: 254 us -> 287 us
    all_to_all x1 -> x0, blocking collectives: 195 us -> none  [per_device(): lax.all_to_all(sent_up, 'ctx', split_axis=0, concat_axis=1, tiled=True)]
    all_to_all x1, waiting for transfers between devices: 0.01 us -> 173 us  [per_device(): lax.all_to_all(sent_down, 'ctx', split_axis=0, concat_axis=1, tiled=True)]
    psum x1 -> x0, waiting for transfers between devices: 140 us -> none  [per_device(): mixed_sum = lax.psum(group_term, 'exp').astype(jnp.float32)]
    all_to_all x1, starting transfers between devices: 5 us -> 36 us  [per_device(): lax.all_to_all(sent_down, 'ctx', split_axis=0, concat_axis=1, tiled=True)]
  transfers between devices with their start and end apart: 34 -> 35, of which waited for: 33 -> 33; matrix products, arithmetic and copies ran while one was open for 2% -> 2% of each run, Pallas kernels for 0% -> 0%
where the time goes in v1:
time: 943 us; the launch traced here: 942 us
  starting transfers between devices  374 us (40%)
  waiting for transfers between devices  287 us (30%)
  blocking collectives  206 us (22%)
  local copies, waits for them, and re-layouts  27.6 us (3%)
  other arithmetic  17.1 us (2%)
  matrix products  14.8 us (2%)
  between operations  14.4 us (2%)
    ppermute x31, starting transfers between devices, shifted(): return lax.ppermute(shard, axis, pairs)  333 us
    all_to_all x1, blocking collectives, per_device(): lax.all_to_all(sent_gate, 'ctx', split_axis=0, concat_axis=1, tiled=True)  206 us
    all_to_all x1, waiting for transfers between devices, per_device(): lax.all_to_all(sent_down, 'ctx', split_axis=0, concat_axis=1, tiled=True)  173 us
    unnamed x3, waiting for transfers between devices  85.8 us
    all_to_all x1, starting transfers between devices, per_device(): lax.all_to_all(sent_down, 'ctx', split_axis=0, concat_axis=1, tiled=True)  36 us
    ppermute x31, waiting for transfers between devices, shifted(): return lax.ppermute(shard, axis, pairs)  27.3 us
  transfers between devices with their start and end apart: 35, of which 33 were waited for; matrix products, arithmetic and copies ran while one was open for 2% of the time, Pallas kernels for 0%

profile of v1, /device:TPU:2, one launch (start us, length us, event | category | flops | bytes accessed | tf_op | source)
XLA Modules:
  0.0 942.1 jit_solution(11643341034983709818)
XLA Ops:
  8.4 2.8 gather_fusion.2
  11.2 2.8 gather_fusion.1
  14.0 2.8 gather_fusion
  16.7 7.7 broadcast_select_fusion.2
  24.4 206.2 %all_to_all.45 = bf16[64,64,448]{2,1,0:T(8,128)(2,1)} all-to-all(bf16[64,64,448]{2,1,0:T(8,128)(2,1)S(1)} %get-tuple-element.53), channel_id=1, replica_groups=mesh['ctx'=32,'exp'=16] {'ctx'}, dimensions={0} | all-to-all | bytes 7340032 | tf_op jit(solution)/shard_map/all_to_all | solution.py:116
  230.6 5.0 all-to-all-start.1
  236.9 364.6 %while.11 = (s32[]{:T(128)}, f32[4,64,128]{2,1,0:T(8,128)S(1)}, f32[1,4]{1,0:T(1,128)S(1)}, f32[4,64,128]{2,1,0:T(8,128)S(1)}, s32[]{:T(128)}, /*index=5*/s32[]{:T(128)}) while((s32[]{:T(128)}, f32[4,64,128]{2,1,0:T(8,128)S(1)}, f32[1,4]{1,0:T(1,128)S(1)}, f32[4,64,128]{2,1,0:T(8,128)S(1)}, s32[]{:T(128)}, ...), condition=%wide.region_2.3_spmd.clone, body=%wide.region_1.2_spmd.clone.sunk | while | flops 163843 | bytes 786567 | solution.py:75
  237.0 2.0 collective-permute-start
  239.0 0.9 collective-permute-done
  240.0 171.1 %collective-permute-start = (bf16[4,64,128]{2,1,0:T(8,128)(2,1)S(1)}, bf16[4,64,128]{2,1,0:T(8,128)(2,1)S(1)}, u32[]{:S(2)}, u32[]{:S(2)}) collective-permute-start(bf16[4,64,128]{2,1,0:T(8,128)(2,1)S(1)} %fusion.64), channel_id=1, source_target_pairs={{0,16},{16,32},{32,48},{48,64},{64,80},{80,96},{96,112},{112,128},... | collective-permute-start | bytes 196616 | tf_op jit(solution)/shard_map/while/body/eval_jaxpr/ppermute | solution.py:15
  412.1 10.2 %collective-permute-start = (bf16[4,64,128]{2,1,0:T(8,128)(2,1)S(1)}, bf16[4,64,128]{2,1,0:T(8,128)(2,1)S(1)}, u32[]{:S(2)}, u32[]{:S(2)}) collective-permute-start(bf16[4,64,128]{2,1,0:T(8,128)(2,1)S(1)} %fusion.64), channel_id=1, source_target_pairs={{0,16},{16,32},{32,48},{48,64},{64,80},{80,96},{96,112},{112,128},... | collective-permute-start | bytes 196616 | tf_op jit(solution)/shard_map/while/body/eval_jaxpr/ppermute | solution.py:15
  423.4 4.8 collective-permute-start
  429.2 4.7 collective-permute-start
  434.9 4.7 collective-permute-start
  440.6 4.7 collective-permute-start
  445.3 0.9 collective-permute-done
  446.3 4.7 collective-permute-start
  451.0 0.9 collective-permute-done
  452.0 4.7 collective-permute-start
  456.7 0.9 collective-permute-done
  457.7 4.7 collective-permute-start
  462.5 0.9 collective-permute-done
  463.5 4.7 collective-permute-start
  468.2 0.9 collective-permute-done
  469.2 4.7 collective-permute-start
  473.9 0.9 collective-permute-done
  474.9 4.7 collective-permute-start
  480.6 4.7 collective-permute-start
  486.3 4.7 collective-permute-start
  492.0 4.9 collective-permute-start
  497.9 5.9 collective-permute-start
  503.8 0.9 collective-permute-done
  504.8 5.9 collective-permute-start
  510.7 0.9 collective-permute-done
  511.7 5.9 collective-permute-start
  517.6 0.9 collective-permute-done
  518.6 5.9 collective-permute-start
  524.5 0.9 collective-permute-done
  525.5 5.9 collective-permute-start
  532.4 5.9 collective-permute-start
  538.4 0.9 collective-permute-done
  539.4 5.9 collective-permute-start
  546.3 5.9 collective-permute-start
  552.2 0.9 collective-permute-done
  553.2 5.9 collective-permute-start
  559.1 0.9 collective-permute-done
  560.1 5.9 collective-permute-start
  567.0 5.9 collective-permute-start
  573.9 5.9 collective-permute-start
  580.9 5.9 collective-permute-start
  587.8 5.9 collective-permute-start
  594.7 5.9 collective-permute-start
  602.5 1.2 convolution_convert_fusion
  603.7 36.0 %all-to-all-start.2 = ((bf16[64,64,448]{2,1,0:T(8,128)(2,1)}), bf16[64,64,448]{2,1,0:T(8,128)(2,1)}, u32[]{:S(2)}, u32[]{:S(2)}) async-start(bf16[64,64,448]{2,1,0:T(8,128)(2,1)} %get-tuple-element.55), calls=%async_computation.2 | async-start | bytes 8388608 | tf_op jit(solution)/shard_map/all_to_all | solution.py:118
  640.2 4.7 copy.39
  644.8 4.9 copy.41
  649.7 173.5 %all-to-all-done.2 = bf16[64,64,448]{2,1,0:T(8,128)(2,1)} async-done(((bf16[64,64,448]{2,1,0:T(8,128)(2,1)}), bf16[64,64,448]{2,1,0:T(8,128)(2,1)}, u32[]{:S(2)}, u32[]{:S(2)}) %all-to-all-start.2) | async-done | bytes 3670048 | tf_op jit(solution)/shard_map/all_to_all | solution.py:118
  823.2 4.6 copy.43
  827.8 5.3 reduce_sum.30
  834.2 4.3 convolution_bitcast_fusion.1
  838.4 7.9 fusion.2
  846.3 1.0 copy.48
  848.1 85.7 %reduce-scatter.4.cloned.1.call-done = bf16[128,128]{1,0:T(8,128)(2,1)} async-done(((bf16[2048,128]{1,0:T(8,128)(2,1)}), bf16[128,128]{1,0:T(8,128)(2,1)}) %reduce-scatter.4.cloned.1.call-update) | async-done | bytes 32784
  933.8 1.5 copy.49
  (148 shorter events, 23.6 us)
Async XLA Ops:
  7.2 1.2 copy-start
  8.4 2.8 copy-start.2
  11.2 2.8 copy-start.3
  230.6 5.1 copy-start.6
  230.6 5.4 copy-start.14
  230.6 5.4 copy-start.12
  230.6 6.1 copy-start.7
  230.6 370.9 %copy-start.8 = (bf16[128,128]{1,0:T(8,128)(2,1)S(1)}, bf16[128,128]{1,0:T(8,128)(2,1)}, u32[]{:S(2)}) copy-start(bf16[128,128]{1,0:T(8,128)(2,1)} %param.22) | copy-start | bytes 98308
  230.6 371.3 %copy-start.15 = (f32[4]{0:T(128)S(1)}, f32[4]{0:T(128)}, u32[]{:S(2)}) copy-start(f32[4]{0:T(128)} %param.25) | copy-start | bytes 52
  230.6 373.1 %all-to-all-start.1 = ((bf16[64,64,448]{2,1,0:T(8,128)(2,1)}), bf16[64,64,448]{2,1,0:T(8,128)(2,1)}, u32[]{:S(2)}, u32[]{:S(2)}) async-start(bf16[64,64,448]{2,1,0:T(8,128)(2,1)} %get-tuple-element.54), calls=%async_computation.1 | async-start | bytes 8388608 | tf_op jit(solution)/shard_map/all_to_all | solution.py:117
  235.7 366.9 %copy-start.5 = (bf16[256,2048]{1,0:T(8,128)(2,1)S(1)}, bf16[256,2048]{1,0:T(8,128)(2,1)}, u32[]{:S(2)}) copy-start(bf16[256,2048]{1,0:T(8,128)(2,1)} %param.26) | copy-start | bytes 3145732
  235.7 366.9 %copy-start.9 = (bf16[128,256]{1,0:T(8,128)(2,1)S(1)}, bf16[128,256]{1,0:T(8,128)(2,1)}, u32[]{:S(2)}) copy-start(bf16[128,256]{1,0:T(8,128)(2,1)} %param.20) | copy-start | bytes 196612
  235.7 592.1 %all-gather.3.cloned.1.call-start = ((), (), s32[]{:S(2)}) async-start(), calls=%async_computation.4 | async-start | bytes 8912896 | tf_op jit(solution)/shard_map/all_gather | solution.py:92
  237.0 2.9 collective-permute-start
  240.0 172.0 %collective-permute-start = (bf16[4,64,128]{2,1,0:T(8,128)(2,1)S(1)}, bf16[4,64,128]{2,1,0:T(8,128)(2,1)S(1)}, u32[]{:S(2)}, u32[]{:S(2)}) collective-permute-start(bf16[4,64,128]{2,1,0:T(8,128)(2,1)S(1)} %fusion.64), channel_id=1, source_target_pairs={{0,16},{16,32},{32,48},{48,64},{64,80},{80,96},{96,112},{112,128},... | collective-permute-start | bytes 196616 | tf_op jit(solution)/shard_map/while/body/eval_jaxpr/ppermute | solution.py:15
  412.1 11.1 %collective-permute-start = (bf16[4,64,128]{2,1,0:T(8,128)(2,1)S(1)}, bf16[4,64,128]{2,1,0:T(8,128)(2,1)S(1)}, u32[]{:S(2)}, u32[]{:S(2)}) collective-permute-start(bf16[4,64,128]{2,1,0:T(8,128)(2,1)S(1)} %fusion.64), channel_id=1, source_target_pairs={{0,16},{16,32},{32,48},{48,64},{64,80},{80,96},{96,112},{112,128},... | collective-permute-start | bytes 196616 | tf_op jit(solution)/shard_map/while/body/eval_jaxpr/ppermute | solution.py:15
  423.4 5.7 collective-permute-start
  429.2 5.6 collective-permute-start
  434.9 5.6 collective-permute-start
  440.6 5.6 collective-permute-start
  446.3 5.6 collective-permute-start
  452.0 5.6 collective-permute-start
  457.7 5.6 collective-permute-start
  463.5 5.6 collective-permute-start
  469.2 5.6 collective-permute-start
  474.9 5.6 collective-permute-start
  480.6 5.6 collective-permute-start
  486.3 5.6 collective-permute-start
  492.0 5.7 collective-permute-start
  497.9 6.8 collective-permute-start
  504.8 6.8 collective-permute-start
  511.7 6.8 collective-permute-start
  518.6 6.8 collective-permute-start
  525.5 6.8 collective-permute-start
  532.4 6.8 collective-permute-start
  539.4 6.8 collective-permute-start
  546.3 6.8 collective-permute-start
  553.2 6.8 collective-permute-start
  560.1 6.8 collective-permute-start
  567.0 6.8 collective-permute-start
  573.9 6.8 collective-permute-start
  580.9 6.8 collective-permute-start
  587.8 6.8 collective-permute-start
  594.7 6.8 collective-permute-start
  603.7 36.2 %copy-start.13 = (s32[32,2]{0,1:T(2,128)S(1)}, s32[32,2]{0,1:T(2,128)}, u32[]{:S(2)}) copy-start(s32[32,2]{0,1:T(2,128)} %param.33) | copy-start | bytes 772
  603.7 219.5 %all-to-all-start.2 = ((bf16[64,64,448]{2,1,0:T(8,128)(2,1)}), bf16[64,64,448]{2,1,0:T(8,128)(2,1)}, u32[]{:S(2)}, u32[]{:S(2)}) async-start(bf16[64,64,448]{2,1,0:T(8,128)(2,1)} %get-tuple-element.55), calls=%async_computation.2 | async-start | bytes 8388608 | tf_op jit(solution)/shard_map/all_to_all | solution.py:118
  639.7 294.1 %reduce-scatter.4.cloned.1.call-start = ((), (), s32[]{:S(2)}) async-start(), calls=%async_computation.5 | async-start | bytes 557056
  827.8 5.3 copy-start.4
  827.8 5.6 copy-start.11
  827.8 5.8 copy-start.10
  838.4 96.9 %copy-start.1 = (bf16[16,64,448]{2,1,0:T(8,128)(2,1)S(1)}, bf16[16,64,448]{2,1,0:T(8,128)(2,1)}, u32[]{:S(2)}) copy-start(bf16[16,64,448]{2,1,0:T(8,128)(2,1)} %param.32) | copy-start | bytes 2752516
Sparse Core Ops, SparseCore 0:
  603.8 110.8 all-gather.2
  847.4 86.3 reduce-scatter.3
